TPU v7x, 32 devices: a whole 2x2x4 slice. The times are simulated.
32 devices in a mesh: row: 8 (over z, core), col: 4 (over y, x).
Axes of the slice: x: 2, y: 2, z: 4, core: 2. Of those that a mesh axis runs over, the one named last changes fastest.
Arguments:
- features: bfloat16 [192, 96, 256], P('row', 'col'), may hold values from -6 to 6
- kernels: bfloat16 [4608, 128], P('row', 'col'), may hold values from -0.125 to 0.125
- out_cotangent: bfloat16 [2, 192, 96, 128], P(None, 'row', 'col'), may hold values from -6 to 6
Outputs:
- branch_maps: bfloat16 [2, 192, 96, 128], P(None, 'row', 'col')
- input_grad: bfloat16 [192, 96, 256], P('row', 'col')
- kernel_grad: float32 [4608, 128], P('row', 'col')
All inputs are finite; a program needn't handle non-finite values.
Results may differ from a plain program's by a relative error of at most 0.001.
Values may be sent and summed in bfloat16 or wider, within the bound.
A program may use at most 64 MiB of HBM per device.

v0:
```python
import jax
import jax.numpy as jnp
from jax import lax
from jax.sharding import PartitionSpec as P

FIRST_SPACING = 12
SECOND_SPACING = 24


def with_halo(x, sides, width):
    for axis, dim in sides:
        size, length = (lax.axis_size(axis), x.shape[dim])
        up = [(i, (i + 1) % size) for i in range(size - 1)]
        down = [(j, i) for i, j in up]
        last = lax.slice_in_dim(x, length - width, length, axis=dim)
        initial = lax.slice_in_dim(x, 0, width, axis=dim)
        before = lax.ppermute(last, axis, up)
        after = lax.ppermute(initial, axis, down)
        x = jnp.concatenate([before, x, after], axis=dim)
    return x


def local(features, kernels, out_cotangent):
    rows_dev = features.shape[0]
    cols_dev = features.shape[1]
    chans = features.shape[2]
    outs_n = out_cotangent.shape[3]
    padding_margin = SECOND_SPACING
    x_ext = with_halo(features, (("row", 0), ("col", 1)), padding_margin)
    g_ext = with_halo(out_cotangent, (("row", 1), ("col", 2)), padding_margin)
    w_cols = lax.all_gather(kernels, "col", axis=1, tiled=True)
    w_full = lax.all_gather(w_cols, "row", axis=0, tiled=True)
    w_blocks = w_full.reshape(2, 9, chans, outs_n)
    pixels = rows_dev * cols_dev
    maps = []
    grads = []
    grad_in = jnp.zeros((pixels, chans), jnp.float32)
    for branch_index, dilation_rate in ((0, FIRST_SPACING), (1, SECOND_SPACING)):
        result = jnp.zeros((pixels, outs_n), jnp.float32)
        g_flat = out_cotangent[branch_index].reshape(pixels, outs_n)
        for kernel_tap in range(9):
            shift_down = (kernel_tap // 3 - 1) * dilation_rate
            shift_across = (kernel_tap % 3 - 1) * dilation_rate
            x_tap = x_ext[
                padding_margin + shift_down : padding_margin + shift_down + rows_dev,
                padding_margin + shift_across : padding_margin + shift_across + cols_dev,
            ].reshape(pixels, chans)
            g_tap = g_ext[
                branch_index,
                padding_margin - shift_down : padding_margin - shift_down + rows_dev,
                padding_margin - shift_across : padding_margin - shift_across + cols_dev,
            ].reshape(pixels, outs_n)
            weight = w_blocks[branch_index, kernel_tap]
            result = result + jnp.dot(x_tap, weight, preferred_element_type=jnp.float32)
            grad_in = grad_in + lax.dot_general(
                g_tap, weight, (((1,), (1,)), ((), ())), preferred_element_type=jnp.float32
            )
            grads.append(
                lax.dot_general(
                    x_tap, g_flat, (((0,), (0,)), ((), ())), preferred_element_type=jnp.float32
                )
            )
        maps.append(result.reshape(rows_dev, cols_dev, outs_n).astype(jnp.bfloat16))
    branch_maps = jnp.stack(maps, 0)
    input_grad = grad_in.reshape(rows_dev, cols_dev, chans).astype(jnp.bfloat16)
    local_grad = jnp.concatenate(grads, 0)
    total_cells = rows_dev * lax.axis_size("row") * cols_dev * lax.axis_size("col")
    scale = 1.0 / jnp.sqrt(jnp.float32(total_cells))
    partial_grad = lax.psum_scatter(local_grad, "row", scatter_dimension=0, tiled=True)
    kernel_grad = lax.psum_scatter(partial_grad, "col", scatter_dimension=1, tiled=True)
    return (branch_maps, input_grad, kernel_grad * scale)


def solution(mesh):
    placed = (P("row", "col", None), P("row", "col"), P(None, "row", "col", None))
    return jax.shard_map(
        local,
        mesh=mesh,
        in_specs=placed,
        out_specs=(P(None, "row", "col", None), P("row", "col", None), P("row", "col")),
        check_vma=False,
    )
```

profile of v0, /device:TPU:0, one launch (start us, length us, event | category | flops | bytes accessed | tf_op | source)
XLA Modules:
  0.0 169.9 jit_solution(2725577153025200455)
XLA Ops:
  7.2 1.4 collective-permute-start.1
  8.7 3.0 %collective-permute-start = (bf16[24,24,256]{2,1,0:T(8,128)(2,1)}, bf16[24,24,256]{2,1,0:T(8,128)(2,1)S(1)}, u32[]{:S(2)}, u32[]{:S(2)}) collective-permute-start(bf16[24,24,256]{2,1,0:T(8,128)(2,1)} %param.3), channel_id=1, source_target_pairs={{0,4},{4,8},{8,12},{12,16},{16,20},{20,24},{24,28},{1,5},{5,9},{9,... | collective-permute-start | bytes 884744 | tf_op jit(solution)/shard_map/ppermute | solution.py:17
  11.7 4.5 %collective-permute-start.4 = (bf16[2,24,24,128]{3,2,1,0:T(8,128)(2,1)}, bf16[2,24,24,128]{3,2,1,0:T(8,128)(2,1)S(1)}, u32[]{:S(2)}, u32[]{:S(2)}) collective-permute-start(bf16[2,24,24,128]{3,2,1,0:T(8,128)(2,1)} %param.5), channel_id=1, source_target_pairs={{0,4},{4,8},{8,12},{12,16},{16,20},{20,24},{24,28},{1,5},{5,9},{9,... | collective-permute-start | bytes 884744 | tf_op jit(solution)/shard_map/ppermute | solution.py:17
  16.3 2.0 %pad_maximum_fusion.6 = (bf16[24,24,256]{2,1,0:T(8,128)(2,1)}, bf16[72,24,256]{2,1,0:T(8,128)(2,1)}, bf16[24,24,256]{2,1,0:T(8,128)(2,1)}) fusion(bf16[24,24,256]{2,1,0:T(8,128)(2,1)} %param.3, bf16[24,24,256]{2,1,0:T(8,128)(2,1)S(1)} %collective-permute-done, bf16[24,24,256]{2,1,0:T(8,128)(2,1)S(1)} %collective-permute-done.1), kind=kLoop, calls=%fused_computation.60 | loop fusion | flops 1179647 | bytes 1769472 | tf_op jit(solution)/shard_map/concatenate | solution.py:19
  19.8 1.3 collective-permute-start.3
  21.1 4.6 %collective-permute-start.2 = (bf16[72,24,256]{2,1,0:T(8,128)(2,1)}, bf16[72,24,256]{2,1,0:T(8,128)(2,1)S(1)}, u32[]{:S(2)}, u32[]{:S(2)}) collective-permute-start(bf16[72,24,256]{2,1,0:T(8,128)(2,1)} %constant_dynamic-update-slice_fusion), channel_id=1, source_target_pairs={{0,1},{1,2},{2,3},{4,5},{5,6},{6,7},{8,9},{9,10},{10,11},{12,13},{... | collective-permute-start | bytes 2654216 | tf_op jit(solution)/shard_map/ppermute | solution.py:17
  25.7 1.3 collective-permute-start.5
  27.0 37.4 %all_gather.6 = bf16[576,128]{0,1:T(8,128)(2,1)S(1)} all-gather(bf16[576,32]{0,1:T(8,128)(2,1)S(1)} %copy-done.47), channel_id=1, replica_groups=mesh['row'=8,'col'=4] {'col'}, dimensions={1}, use_global_device_ids=true | all-gather | bytes 184320 | tf_op jit(solution)/shard_map/all_gather | solution.py:31
  67.7 6.1 %collective-permute-start.7 = (bf16[2,72,24,128]{3,2,1,0:T(8,128)(2,1)}, bf16[2,72,24,128]{3,2,1,0:T(8,128)(2,1)}, u32[]{:S(2)}, u32[]{:S(2)}) collective-permute-start(bf16[2,72,24,128]{3,2,1,0:T(8,128)(2,1)} %constant_dynamic-update-slice_fusion.3), channel_id=1, source_target_pairs={{0,1},{1,2},{2,3},{4,5},{5,6},{6,7},{8,9},{9,10},{10,11},{12,13},{... | collective-permute-start | bytes 2654216 | tf_op jit(solution)/shard_map/ppermute | solution.py:17
  73.8 1.3 collective-permute-start.6
  75.9 2.4 %pad_maximum_fusion.3 = (bf16[24,24,256]{2,1,0:T(8,128)(2,1)S(1)}, bf16[24,24,256]{2,1,0:T(8,128)(2,1)S(1)}, bf16[24,24,256]{2,1,0:T(8,128)(2,1)S(1)}, bf16[24,2...) fusion(bf16[72,24,256]{2,1,0:T(8,128)(2,1)S(1)} %collective-per, ...), kind=kLoop, calls=%fused_computation.57 | loop fusion | flops 3538944 | bytes 7962624 | tf_op jit(solution)/shard_map/slice | solution.py:44
  78.4 1.3 convolution_dynamic-update-slice_fusion.17
  79.8 1.0 convolution_dynamic-update-slice_fusion.16
  81.7 0.9 convolution_dynamic-update-slice_fusion.14
  83.6 0.9 convolution_dynamic-update-slice_fusion.12
  85.5 1.0 convolution_dynamic-update-slice_fusion.10
  86.4 1.0 convolution_dynamic-update-slice_fusion.9
  89.3 1.0 convolution_dynamic-update-slice_fusion.6
  91.2 1.0 convolution_dynamic-update-slice_fusion.4
  93.1 1.0 convolution_dynamic-update-slice_fusion.2
  95.0 0.9 convolution_dynamic-update-slice_fusion
  96.0 17.6 %collective-permute-done.6 = bf16[2,72,24,128]{3,2,1,0:T(8,128)(2,1)} collective-permute-done((bf16[2,72,24,128]{3,2,1,0:T(8,128)(2,1)}, bf16[2,72,24,128]{3,2,1,0:T(8,128)(2,1)}, u32[]{:S(2)}, u32[]{:S(2)}) %collective-permute-start.6) | collective-permute-done | bytes 884768 | tf_op jit(solution)/shard_map/ppermute | solution.py:18
  113.6 2.9 %pad_maximum_fusion.12 = (bf16[1,24,24,128]{3,2,1,0:T(8,128)(2,1)}, bf16[1,24,24,128]{3,2,1,0:T(8,128)(2,1)}, bf16[1,24,24,128]{3,2,1,0:T(8,128)(2,1)}, bf16[1,2...) fusion(bf16[2,72,24,128]{3,2,1,0:T(8,128)(2,1)} %constant_dynam, ...), kind=kLoop, calls=%fused_computation.66 | loop fusion | flops 1769472 | bytes 5308416 | tf_op jit(solution)/shard_map/slice | solution.py:48
  116.5 1.2 fusion.51
  117.7 1.1 fusion.36
  123.4 1.1 fusion.54
  125.9 1.0 fusion.52
  131.9 3.4 %reduce-scatter.5.cloned.1.call-done = f32[576,128]{1,0:T(8,128)} async-done(((f32[4608,128]{1,0:T(8,128)}), f32[576,128]{1,0:T(8,128)}) %reduce-scatter.5.cloned.1.call-update) | async-done | bytes 294928 | tf_op jit(solution)/shard_map/reduce_scatter | solution.py:69
  135.3 1.9 %copy.11 = f32[576,128]{0,1:T(8,128)} copy(f32[576,128]{1,0:T(8,128)} %reduce-scatter.5.cloned.1.call-done) | data formatting | bytes 589824
  138.2 1.0 fusion.14
  139.2 22.3 %reduce-scatter.7.cloned.1.call-done = f32[32,576]{1,0:T(8,128)} async-done(((f32[128,576]{1,0:T(8,128)}), f32[32,576]{1,0:T(8,128)}) %reduce-scatter.7.cloned.1.call-update) | async-done | bytes 73744
  161.6 1.0 copy.12
  (159 shorter events, 25.6 us)
Async XLA Ops:
  7.2 11.2 %copy-start = (bf16[24,24,256]{2,1,0:T(8,128)(2,1)S(1)}, bf16[24,24,256]{2,1,0:T(8,128)(2,1)}, u32[]{:S(2)}) copy-start(bf16[24,24,256]{2,1,0:T(8,128)(2,1)} %param.3) | copy-start | bytes 884740
  7.2 18.6 %copy-start.27 = (bf16[2,24,24,128]{3,2,1,0:T(8,128)(2,1)S(1)}, bf16[2,24,24,128]{3,2,1,0:T(8,128)(2,1)}, u32[]{:S(2)}) copy-start(bf16[2,24,24,128]{3,2,1,0:T(8,128)(2,1)} %param.5) | copy-start | bytes 884740
  7.2 19.9 %copy-start.47 = (bf16[576,32]{0,1:T(8,128)(2,1)S(1)}, bf16[576,32]{0,1:T(8,128)(2,1)}, u32[]{:S(2)}) copy-start(bf16[576,32]{0,1:T(8,128)(2,1)} %param.4) | copy-start | bytes 110596
  7.2 109.3 %all-gather.2.cloned.1.call-start = ((), (), s32[]{:S(2)}) async-start(), calls=%async_computation.2 | async-start | bytes 1327104 | tf_op jit(solution)/shard_map/all_gather | solution.py:32
  7.2 9.0 %collective-permute-start.1 = (bf16[24,24,256]{2,1,0:T(8,128)(2,1)}, bf16[24,24,256]{2,1,0:T(8,128)(2,1)S(1)}, u32[]{:S(2)}, u32[]{:S(2)}) collective-permute-start(bf16[24,24,256]{2,1,0:T(8,128)(2,1)} %param.3), channel_id=1, source_target_pairs={{4,0},{8,4},{12,8},{16,12},{20,16},{24,20},{28,24},{5,1},{9,5},{13... | collective-permute-start | bytes 884744 | tf_op jit(solution)/shard_map/ppermute | solution.py:18
  8.7 7.6 %collective-permute-start = (bf16[24,24,256]{2,1,0:T(8,128)(2,1)}, bf16[24,24,256]{2,1,0:T(8,128)(2,1)S(1)}, u32[]{:S(2)}, u32[]{:S(2)}) collective-permute-start(bf16[24,24,256]{2,1,0:T(8,128)(2,1)} %param.3), channel_id=1, source_target_pairs={{0,4},{4,8},{8,12},{12,16},{16,20},{20,24},{24,28},{1,5},{5,9},{9,... | collective-permute-start | bytes 884744 | tf_op jit(solution)/shard_map/ppermute | solution.py:17
  11.7 53.6 %collective-permute-start.4 = (bf16[2,24,24,128]{3,2,1,0:T(8,128)(2,1)}, bf16[2,24,24,128]{3,2,1,0:T(8,128)(2,1)S(1)}, u32[]{:S(2)}, u32[]{:S(2)}) collective-permute-start(bf16[2,24,24,128]{3,2,1,0:T(8,128)(2,1)} %param.5), channel_id=1, source_target_pairs={{0,4},{4,8},{8,12},{12,16},{16,20},{20,24},{24,28},{1,5},{5,9},{9,... | collective-permute-start | bytes 884744 | tf_op jit(solution)/shard_map/ppermute | solution.py:17
  19.8 56.1 %collective-permute-start.3 = (bf16[72,24,256]{2,1,0:T(8,128)(2,1)}, bf16[72,24,256]{2,1,0:T(8,128)(2,1)S(1)}, u32[]{:S(2)}, u32[]{:S(2)}) collective-permute-start(bf16[72,24,256]{2,1,0:T(8,128)(2,1)} %constant_dynamic-update-slice_fusion), channel_id=1, source_target_pairs={{1,0},{2,1},{3,2},{5,4},{6,5},{7,6},{9,8},{10,9},{11,10},{13,12},{... | collective-permute-start | bytes 2654216 | tf_op jit(solution)/shard_map/ppermute | solution.py:18
  21.1 54.8 %collective-permute-start.2 = (bf16[72,24,256]{2,1,0:T(8,128)(2,1)}, bf16[72,24,256]{2,1,0:T(8,128)(2,1)S(1)}, u32[]{:S(2)}, u32[]{:S(2)}) collective-permute-start(bf16[72,24,256]{2,1,0:T(8,128)(2,1)} %constant_dynamic-update-slice_fusion), channel_id=1, source_target_pairs={{0,1},{1,2},{2,3},{4,5},{5,6},{6,7},{8,9},{9,10},{10,11},{12,13},{... | collective-permute-start | bytes 2654216 | tf_op jit(solution)/shard_map/ppermute | solution.py:17
  25.7 41.2 %collective-permute-start.5 = (bf16[2,24,24,128]{3,2,1,0:T(8,128)(2,1)S(1)}, bf16[2,24,24,128]{3,2,1,0:T(8,128)(2,1)S(1)}, u32[]{:S(2)}, u32[]{:S(2)}) collective-permute-start(bf16[2,24,24,128]{3,2,1,0:T(8,128)(2,1)S(1)} %copy-done.27), channel_id=1, source_target_pairs={{4,0},{8,4},{12,8},{16,12},{20,16},{24,20},{28,24},{5,1},{9,5},{13... | collective-permute-start | bytes 884744 | tf_op jit(solution)/shard_map/ppermute | solution.py:18
  65.3 70.0 %reduce-scatter.5.cloned.1.call-start = ((), (), s32[]{:S(2)}) async-start(), calls=%async_computation.3 | async-start | bytes 2654208 | tf_op jit(solution)/shard_map/reduce_scatter | solution.py:69
  67.7 28.3 %collective-permute-start.7 = (bf16[2,72,24,128]{3,2,1,0:T(8,128)(2,1)}, bf16[2,72,24,128]{3,2,1,0:T(8,128)(2,1)}, u32[]{:S(2)}, u32[]{:S(2)}) collective-permute-start(bf16[2,72,24,128]{3,2,1,0:T(8,128)(2,1)} %constant_dynamic-update-slice_fusion.3), channel_id=1, source_target_pairs={{0,1},{1,2},{2,3},{4,5},{5,6},{6,7},{8,9},{9,10},{10,11},{12,13},{... | collective-permute-start | bytes 2654216 | tf_op jit(solution)/shard_map/ppermute | solution.py:17
  73.8 39.8 %collective-permute-start.6 = (bf16[2,72,24,128]{3,2,1,0:T(8,128)(2,1)}, bf16[2,72,24,128]{3,2,1,0:T(8,128)(2,1)}, u32[]{:S(2)}, u32[]{:S(2)}) collective-permute-start(bf16[2,72,24,128]{3,2,1,0:T(8,128)(2,1)} %constant_dynamic-update-slice_fusion.3), channel_id=1, source_target_pairs={{1,0},{2,1},{3,2},{5,4},{6,5},{7,6},{9,8},{10,9},{11,10},{13,12},{... | collective-permute-start | bytes 2654216 | tf_op jit(solution)/shard_map/ppermute | solution.py:18
  75.9 3.8 %copy-start.25 = (bf16[24,24,256]{2,1,0:T(8,128)(2,1)S(1)}, bf16[24,24,256]{2,1,0:T(8,128)(2,1)}, u32[]{:S(2)}) copy-start(bf16[24,24,256]{2,1,0:T(8,128)(2,1)} %get-tuple-element.48) | copy-start | bytes 884740
  78.3 5.2 %copy-start.4 = (bf16[24,24,256]{2,1,0:T(8,128)(2,1)}, bf16[24,24,256]{2,1,0:T(8,128)(2,1)S(1)}, u32[]{:S(2)}) copy-start(bf16[24,24,256]{2,1,0:T(8,128)(2,1)S(1)} %get-tuple-element.35) | copy-start | bytes 884740
  78.3 5.2 %copy-start.14 = (bf16[24,24,256]{2,1,0:T(8,128)(2,1)}, bf16[24,24,256]{2,1,0:T(8,128)(2,1)S(1)}, u32[]{:S(2)}) copy-start(bf16[24,24,256]{2,1,0:T(8,128)(2,1)S(1)} %get-tuple-element.34) | copy-start | bytes 884740
  78.3 5.2 %copy-start.2 = (bf16[24,24,256]{2,1,0:T(8,128)(2,1)}, bf16[24,24,256]{2,1,0:T(8,128)(2,1)S(1)}, u32[]{:S(2)}) copy-start(bf16[24,24,256]{2,1,0:T(8,128)(2,1)S(1)} %get-tuple-element.18) | copy-start | bytes 884740
  78.4 6.2 %copy-start.16 = (bf16[24,24,256]{2,1,0:T(8,128)(2,1)}, bf16[24,24,256]{2,1,0:T(8,128)(2,1)S(1)}, u32[]{:S(2)}) copy-start(bf16[24,24,256]{2,1,0:T(8,128)(2,1)S(1)} %get-tuple-element.33) | copy-start | bytes 884740
  78.4 8.1 %copy-start.18 = (bf16[24,24,256]{2,1,0:T(8,128)(2,1)}, bf16[24,24,256]{2,1,0:T(8,128)(2,1)S(1)}, u32[]{:S(2)}) copy-start(bf16[24,24,256]{2,1,0:T(8,128)(2,1)S(1)} %get-tuple-element.20) | copy-start | bytes 884740
  78.4 10.9 %copy-start.6 = (bf16[24,24,256]{2,1,0:T(8,128)(2,1)}, bf16[24,24,256]{2,1,0:T(8,128)(2,1)S(1)}, u32[]{:S(2)}) copy-start(bf16[24,24,256]{2,1,0:T(8,128)(2,1)S(1)} %get-tuple-element.41) | copy-start | bytes 884740
  78.4 11.8 %copy-start.10 = (bf16[24,24,256]{2,1,0:T(8,128)(2,1)}, bf16[24,24,256]{2,1,0:T(8,128)(2,1)S(1)}, u32[]{:S(2)}) copy-start(bf16[24,24,256]{2,1,0:T(8,128)(2,1)S(1)} %get-tuple-element.37) | copy-start | bytes 884740
  78.4 12.8 %copy-start.20 = (bf16[24,24,256]{2,1,0:T(8,128)(2,1)}, bf16[24,24,256]{2,1,0:T(8,128)(2,1)S(1)}, u32[]{:S(2)}) copy-start(bf16[24,24,256]{2,1,0:T(8,128)(2,1)S(1)} %get-tuple-element.19) | copy-start | bytes 884740
  78.4 14.7 %copy-start.12 = (bf16[24,24,256]{2,1,0:T(8,128)(2,1)}, bf16[24,24,256]{2,1,0:T(8,128)(2,1)S(1)}, u32[]{:S(2)}) copy-start(bf16[24,24,256]{2,1,0:T(8,128)(2,1)S(1)} %get-tuple-element.36) | copy-start | bytes 884740
  78.4 16.5 %copy-start.8 = (bf16[24,24,256]{2,1,0:T(8,128)(2,1)}, bf16[24,24,256]{2,1,0:T(8,128)(2,1)S(1)}, u32[]{:S(2)}) copy-start(bf16[24,24,256]{2,1,0:T(8,128)(2,1)S(1)} %get-tuple-element.39) | copy-start | bytes 884740
  81.7 3.8 %copy-start.24 = (bf16[24,24,256]{2,1,0:T(8,128)(2,1)S(1)}, bf16[24,24,256]{2,1,0:T(8,128)(2,1)}, u32[]{:S(2)}) copy-start(bf16[24,24,256]{2,1,0:T(8,128)(2,1)} %get-tuple-element.50) | copy-start | bytes 884740
  84.5 3.8 %copy-start.23 = (bf16[24,24,256]{2,1,0:T(8,128)(2,1)S(1)}, bf16[24,24,256]{2,1,0:T(8,128)(2,1)}, u32[]{:S(2)}) copy-start(bf16[24,24,256]{2,1,0:T(8,128)(2,1)} %copy-done.22) | copy-start | bytes 884740
  95.9 65.6 %reduce-scatter.7.cloned.1.call-start = ((), (), s32[]{:S(2)}) async-start(), calls=%async_computation.4 | async-start | bytes 409600
  131.5 5.8 %copy-start.34 = (bf16[576,128]{1,0:T(8,128)(2,1)S(1)}, bf16[576,128]{1,0:T(8,128)(2,1)}, u32[]{:S(2)}) copy-start(bf16[576,128]{1,0:T(8,128)(2,1)} %fusion.27) | copy-start | bytes 442372
  131.9 6.1 %copy-start.38 = (bf16[1,24,24,128]{3,2,1,0:T(8,128)(2,1)S(1)}, bf16[1,24,24,128]{3,2,1,0:T(8,128)(2,1)}, u32[]{:S(2)}) copy-start(bf16[1,24,24,128]{3,2,1,0:T(8,128)(2,1)} %get-tuple-element.31) | copy-start | bytes 442372
  131.9 6.3 %copy-start.28 = (f32[576,256]{1,0:T(8,128)S(1)}, f32[576,256]{1,0:T(8,128)}, u32[]{:S(2)}) copy-start(f32[576,256]{1,0:T(8,128)} %fusion.54) | copy-start | bytes 1769476
  131.9 6.3 %copy-start.29 = (f32[576,256]{1,0:T(8,128)S(1)}, f32[576,256]{1,0:T(8,128)}, u32[]{:S(2)}) copy-start(f32[576,256]{1,0:T(8,128)} %fusion.52) | copy-start | bytes 1769476
  131.9 6.3 %copy-start.35 = (bf16[1,24,24,128]{3,2,1,0:T(8,128)(2,1)S(1)}, bf16[1,24,24,128]{3,2,1,0:T(8,128)(2,1)}, u32[]{:S(2)}) copy-start(bf16[1,24,24,128]{3,2,1,0:T(8,128)(2,1)} %get-tuple-element.24) | copy-start | bytes 442372
  (27 other events, 33.8 us)
Sparse Core Ops, SparseCore 0:
  65.4 26.3 all-gather.1
  96.1 39.2 reduce-scatter.4
  138.1 23.4 reduce-scatter.6
where the time goes:
time: 171 us; the launch traced here: 170 us
  waiting for transfers between devices  43.4 us (25%)
  blocking collectives  37.4 us (22%)
  matrix products  30.7 us (18%)
  starting transfers between devices  23.7 us (14%)
  between operations  14.5 us (8%)
  local copies, waits for them, and re-layouts  11.2 us (7%)
  other arithmetic  8.92 us (5%)
    all_gather x1, blocking collectives, local(): w_cols = lax.all_gather(kernels, 'col', axis=1, tiled=True)  37.4 us
    unnamed x4, waiting for transfers between devices  22.4 us
    ppermute x4, starting transfers between devices, with_halo(): before = lax.ppermute(last, axis, up)  18.3 us
    ppermute x4, waiting for transfers between devices, with_halo(): after = lax.ppermute(initial, axis, down)  17.6 us
    dot_general x18, matrix products, local(): lax.dot_general(x_tap, g_flat, (((0,), (0,)), ((), ())), preferred_elemen...  17.4 us
    unnamed x102, local copies, waits for them, and re-layouts  8.93 us
    dot_general x18, matrix products, local(): lax.dot_general(g_tap, weight, (((1,), (1,)), ((), ())), preferred_elemen...  6.7 us
    dot_general x18, matrix products, local(): result = result + jnp.dot(x_tap, weight, preferred_element_type=jnp.float32)  6.55 us
  transfers between devices with their start and end apart: 11, of which 3 were waited for; matrix products, arithmetic and copies ran while one was open for 26% of the time, Pallas kernels for 0%

commit v1 on v0

--- a/solution.py
+++ b/solution.py
@@ -5,6 +5,18 @@
 
 FIRST_SPACING = 12
 SECOND_SPACING = 24
+
+
+def collect(x, axis, dim):
+    ways, here, step = (lax.axis_size(axis), lax.axis_index(axis), x.shape[dim])
+    line, have = (x, 1)
+    while have < ways:
+        line = jnp.concatenate(
+            [line, lax.ppermute(line, axis, [(d, (d - have) % ways) for d in range(ways)])],
+            axis=dim,
+        )
+        have = 2 * have
+    return jnp.roll(line, here * step, axis=dim)
 
 
 def with_halo(x, sides, width):
@@ -28,7 +40,7 @@
     padding_margin = SECOND_SPACING
     x_ext = with_halo(features, (("row", 0), ("col", 1)), padding_margin)
     g_ext = with_halo(out_cotangent, (("row", 1), ("col", 2)), padding_margin)
-    w_cols = lax.all_gather(kernels, "col", axis=1, tiled=True)
+    w_cols = collect(kernels, "col", 1)
     w_full = lax.all_gather(w_cols, "row", axis=0, tiled=True)
     w_blocks = w_full.reshape(2, 9, chans, outs_n)
     pixels = rows_dev * cols_dev

time: 171 us -> 161 us (0.942)
  blocking collectives: 37.4 us -> 0 us
  starting transfers between devices: 23.7 us -> 38.6 us
  matrix products: 30.7 us -> 39.1 us
  local copies, waits for them, and re-layouts: 11.2 us -> 13.9 us
    all_gather x1 -> x0, blocking collectives: 37.4 us -> none  [local(): w_cols = lax.all_gather(kernels, 'col', axis=1, tiled=True)]
    ppermute x4, starting transfers between devices: 18.3 us -> 28.5 us  [with_halo(): before = lax.ppermute(last, axis, up)]
    dot_general x18, matrix products: 6.7 us -> 15.8 us  [local(): lax.dot_general(g_tap, weight, (((1,), (1,)), ((), ())), preferred_elemen...]
    ppermute x0 -> x2, waiting for transfers between devices: none -> 4.46 us  [collect(): lax.ppermute(line, axis, [(d, (d - have) % ways) for d in range(ways)])]
    ppermute x4, waiting for transfers between devices: 17.6 us -> 22 us  [with_halo(): after = lax.ppermute(initial, axis, down)]
    ppermute x0 -> x2, starting transfers between devices: none -> 4.45 us  [collect(): lax.ppermute(line, axis, [(d, (d - have) % ways) for d in range(ways)])]
    unnamed x4, waiting for transfers between devices: 22.4 us -> 18.2 us
    reduce_scatter x1, waiting for transfers between devices: 3.43 us -> 0.01 us  [local(): lax.psum_scatter(local_grad, 'row', scatter_dimension=0, tiled=True)]
  transfers between devices with their start and end apart: 11 -> 13, of which waited for: 3 -> 3; matrix products, arithmetic and copies ran while one was open for 26% -> 36% of each run, Pallas kernels for 0% -> 0%
where the time goes in v1:
time: 161 us; the launch traced here: 160 us
  waiting for transfers between devices  44.7 us (28%)
  matrix products  39.1 us (24%)
  starting transfers between devices  38.6 us (24%)
  between operations  14.4 us (9%)
  local copies, waits for them, and re-layouts  13.9 us (9%)
  other arithmetic  9.54 us (6%)
    ppermute x4, starting transfers between devices, with_halo(): before = lax.ppermute(last, axis, up)  28.5 us
    ppermute x4, waiting for transfers between devices, with_halo(): after = lax.ppermute(initial, axis, down)  22 us
    unnamed x4, waiting for transfers between devices  18.2 us
    dot_general x18, matrix products, local(): lax.dot_general(x_tap, g_flat, (((0,), (0,)), ((), ())), preferred_elemen...  17.4 us
    dot_general x18, matrix products, local(): lax.dot_general(g_tap, weight, (((1,), (1,)), ((), ())), preferred_elemen...  15.8 us
    unnamed x95, local copies, waits for them, and re-layouts  8.75 us
    dot_general x18, matrix products, local(): result = result + jnp.dot(x_tap, weight, preferred_element_type=jnp.float32)  5.87 us
    ppermute x4, starting transfers between devices, with_halo(): after = lax.ppermute(initial, axis, down)  5.26 us
  transfers between devices with their start and end apart: 13, of which 3 were waited for; matrix products, arithmetic and copies ran while one was open for 36% of the time, Pallas kernels for 0%

profile of v1, /device:TPU:0, one launch (start us, length us, event | category | flops | bytes accessed | tf_op | source)
XLA Modules:
  0.0 160.3 jit_solution(14531792034997506399)
XLA Ops:
  7.2 1.4 collective-permute-start.1
  8.7 3.1 %collective-permute-start = (bf16[24,24,256]{2,1,0:T(8,128)(2,1)}, bf16[24,24,256]{2,1,0:T(8,128)(2,1)S(1)}, u32[]{:S(2)}, u32[]{:S(2)}) collective-permute-start(bf16[24,24,256]{2,1,0:T(8,128)(2,1)} %param.3), channel_id=1, source_target_pairs={{0,4},{4,8},{8,12},{12,16},{16,20},{20,24},{24,28},{1,5},{5,9},{9,... | collective-permute-start | bytes 884744 | tf_op jit(solution)/shard_map/ppermute | solution.py:29
  12.6 3.9 %collective-permute-start.3 = (bf16[576,32]{1,0:T(8,128)(2,1)S(1)}, bf16[576,32]{1,0:T(8,128)(2,1)S(1)}, u32[]{:S(2)}, u32[]{:S(2)}) collective-permute-start(bf16[576,32]{1,0:T(8,128)(2,1)S(1)} %copy.14), channel_id=1, source_target_pairs={{0,3},{1,0},{2,1},{3,2},{4,7},{5,4},{6,5},{7,6},{8,11},{9,8},{10,9... | collective-permute-start | bytes 110600 | tf_op jit(solution)/shard_map/ppermute | solution.py:15
  16.6 2.8 %collective-permute-start.6 = (bf16[2,24,24,128]{3,2,1,0:T(8,128)(2,1)}, bf16[2,24,24,128]{3,2,1,0:T(8,128)(2,1)S(1)}, u32[]{:S(2)}, u32[]{:S(2)}) collective-permute-start(bf16[2,24,24,128]{3,2,1,0:T(8,128)(2,1)} %param.5), channel_id=1, source_target_pairs={{0,4},{4,8},{8,12},{12,16},{16,20},{20,24},{24,28},{1,5},{5,9},{9,... | collective-permute-start | bytes 884744 | tf_op jit(solution)/shard_map/ppermute | solution.py:29
  19.4 2.0 %pad_maximum_fusion.6 = (bf16[24,24,256]{2,1,0:T(8,128)(2,1)}, bf16[72,24,256]{2,1,0:T(8,128)(2,1)}, bf16[24,24,256]{2,1,0:T(8,128)(2,1)}) fusion(bf16[24,24,256]{2,1,0:T(8,128)(2,1)} %param.3, bf16[24,24,256]{2,1,0:T(8,128)(2,1)S(1)} %collective-permute-done, bf16[24,24,256]{2,1,0:T(8,128)(2,1)S(1)} %collective-permute-done.1), kind=kLoop, calls=%fused_computation.68 | loop fusion | flops 1179647 | bytes 1769472 | tf_op jit(solution)/shard_map/concatenate | solution.py:31
  22.9 1.3 collective-permute-start.5
  24.2 4.6 %collective-permute-start.2 = (bf16[72,24,256]{2,1,0:T(8,128)(2,1)}, bf16[72,24,256]{2,1,0:T(8,128)(2,1)S(1)}, u32[]{:S(2)}, u32[]{:S(2)}) collective-permute-start(bf16[72,24,256]{2,1,0:T(8,128)(2,1)} %constant_dynamic-update-slice_fusion), channel_id=1, source_target_pairs={{0,1},{1,2},{2,3},{4,5},{5,6},{6,7},{8,9},{9,10},{10,11},{12,13},{... | collective-permute-start | bytes 2654216 | tf_op jit(solution)/shard_map/ppermute | solution.py:29
  30.1 1.3 collective-permute-start.7
  31.5 4.5 %collective-permute-done.4 = bf16[576,64]{1,0:T(8,128)(2,1)} collective-permute-done((bf16[576,64]{1,0:T(8,128)(2,1)}, bf16[576,64]{1,0:T(8,128)(2,1)}, u32[]{:S(2)}, u32[]{:S(2)}) %collective-permute-start.4) | collective-permute-done | bytes 73760 | tf_op jit(solution)/shard_map/ppermute | solution.py:15
  35.9 2.0 %concatenate.56 = bf16[576,256]{1,0:T(8,128)(2,1)} concatenate(bf16[576,32]{1,0:T(8,128)(2,1)S(1)} %copy.14, bf16[576,32]{1,0:T(8,128)(2,1)S(1)} %collective-permute-done.3, bf16[576,64]{1,0:T(8,128)(2,1)} %collective-permute-done.4, bf16[576,32]{1,0:T(8,128)(2,1)S(1)} %copy.14, bf16[576,32]{1,0:T(8,128)(2,1)S(1)} %collective-permute-done.3, bf16[576,64]{1,0:T(8,128)(2,1)} %collective-permute-done.4), dimensions={1} | concatenate | bytes 589824 | tf_op jit(solution)/shard_map/jit(_roll_dynamic)/concatenate | solution.py:19
  37.9 1.7 %constant_dynamic-slice_fusion = bf16[576,128]{1,0:T(8,128)(2,1)} fusion(bf16[576,256]{1,0:T(8,128)(2,1)} %concatenate.56, s32[]{:T(128)S(6)} %select_n.14), kind=kLoop, calls=%fused_computation.128 | loop fusion | bytes 294916 | tf_op jit(solution)/shard_map/jit(_roll_dynamic)/dynamic_slice | solution.py:19
  42.0 18.1 %collective-permute-start.9 = (bf16[2,72,24,128]{3,2,1,0:T(8,128)(2,1)}, bf16[2,72,24,128]{3,2,1,0:T(8,128)(2,1)}, u32[]{:S(2)}, u32[]{:S(2)}) collective-permute-start(bf16[2,72,24,128]{3,2,1,0:T(8,128)(2,1)} %constant_dynamic-update-slice_fusion.3), channel_id=1, source_target_pairs={{0,1},{1,2},{2,3},{4,5},{5,6},{6,7},{8,9},{9,10},{10,11},{12,13},{... | collective-permute-start | bytes 2654216 | tf_op jit(solution)/shard_map/ppermute | solution.py:29
  60.1 1.3 collective-permute-start.8
  62.2 2.3 %pad_maximum_fusion.3 = (bf16[24,24,256]{2,1,0:T(8,128)(2,1)S(1)}, bf16[24,24,256]{2,1,0:T(8,128)(2,1)S(1)}, bf16[24,24,256]{2,1,0:T(8,128)(2,1)S(1)}, bf16[24,2...) fusion(bf16[72,24,256]{2,1,0:T(8,128)(2,1)S(1)} %collective-per, ...), kind=kLoop, calls=%fused_computation.65 | loop fusion | flops 3538944 | bytes 7962624 | tf_op jit(solution)/shard_map/slice | solution.py:56
  64.6 1.3 convolution_dynamic-update-slice_fusion.17
  82.3 22.0 %collective-permute-done.8 = bf16[2,72,24,128]{3,2,1,0:T(8,128)(2,1)} collective-permute-done((bf16[2,72,24,128]{3,2,1,0:T(8,128)(2,1)}, bf16[2,72,24,128]{3,2,1,0:T(8,128)(2,1)}, u32[]{:S(2)}, u32[]{:S(2)}) %collective-permute-start.8) | collective-permute-done | bytes 884768 | tf_op jit(solution)/shard_map/ppermute | solution.py:30
  104.3 2.8 %pad_maximum_fusion.12 = (bf16[1,24,24,128]{3,2,1,0:T(8,128)(2,1)}, bf16[1,24,24,128]{3,2,1,0:T(8,128)(2,1)}, bf16[1,24,24,128]{3,2,1,0:T(8,128)(2,1)}, bf16[1,2...) fusion(bf16[2,72,24,128]{3,2,1,0:T(8,128)(2,1)} %constant_dynam, ...), kind=kLoop, calls=%fused_computation.74 | loop fusion | flops 1769472 | bytes 5308416 | tf_op jit(solution)/shard_map/slice | solution.py:60
  107.2 1.2 convolution_bitcast_fusion.5
  108.4 1.1 convolution_bitcast_fusion.7
  114.4 1.0 convolution_bitcast_fusion
  115.4 1.1 convolution_bitcast_fusion.2
  116.7 1.1 fusion.41
  117.8 1.1 fusion.52
  118.9 1.1 fusion.48
  119.9 1.1 fusion.44
  121.0 1.1 fusion.37
  122.3 1.0 fusion.50
  123.3 1.1 fusion.46
  125.9 1.1 fusion.2
  127.1 1.9 %copy.17 = f32[576,128]{0,1:T(8,128)} copy(f32[576,128]{1,0:T(8,128)} %reduce-scatter.5.cloned.1.call-done) | data formatting | bytes 589824
  130.1 3.6 %fusion.15 = bf16[576,256]{1,0:T(8,128)(2,1)} fusion(f32[576,256]{1,0:T(8,128)} %fusion.52, f32[576,256]{1,0:T(8,128)S(1)} %copy-done.28, f32[576,256]{1,0:T(8,128)} %fusion.50, f32[576,256]{1,0:T(8,128)} %fusion.48, f32[576,256]{1,0:T(8,128)S(1)} %convolution_bitcast_fusion.1, f32[576,256]{1,0:T(8,128)} %fusion.46, f32[576,256]{1,0:T(8,128)} %fusion.44, ...), kind=kOutput, calls=%fused_computation.21 | convolution fusion | flops 39813120 | bytes 8175616 | tf_op jit(solution)/shard_map/dot_general | solution.py:67
  133.7 18.2 %reduce-scatter.7.cloned.1.call-done = f32[32,576]{1,0:T(8,128)} async-done(((f32[128,576]{1,0:T(8,128)}), f32[32,576]{1,0:T(8,128)}) %reduce-scatter.7.cloned.1.call-update) | async-done | bytes 73744
  (157 shorter events, 32.9 us)
Async XLA Ops:
  7.2 14.3 %copy-start = (bf16[24,24,256]{2,1,0:T(8,128)(2,1)S(1)}, bf16[24,24,256]{2,1,0:T(8,128)(2,1)}, u32[]{:S(2)}) copy-start(bf16[24,24,256]{2,1,0:T(8,128)(2,1)} %param.3) | copy-start | bytes 884740
  7.2 100.0 %all-gather.2.cloned.1.call-start = ((), (), s32[]{:S(2)}) async-start(), calls=%async_computation.2 | async-start | bytes 1327104 | tf_op jit(solution)/shard_map/all_gather | solution.py:44
  7.2 12.2 %collective-permute-start.1 = (bf16[24,24,256]{2,1,0:T(8,128)(2,1)}, bf16[24,24,256]{2,1,0:T(8,128)(2,1)S(1)}, u32[]{:S(2)}, u32[]{:S(2)}) collective-permute-start(bf16[24,24,256]{2,1,0:T(8,128)(2,1)} %param.3), channel_id=1, source_target_pairs={{4,0},{8,4},{12,8},{16,12},{20,16},{24,20},{28,24},{5,1},{9,5},{13... | collective-permute-start | bytes 884744 | tf_op jit(solution)/shard_map/ppermute | solution.py:30
  8.7 10.8 %collective-permute-start = (bf16[24,24,256]{2,1,0:T(8,128)(2,1)}, bf16[24,24,256]{2,1,0:T(8,128)(2,1)S(1)}, u32[]{:S(2)}, u32[]{:S(2)}) collective-permute-start(bf16[24,24,256]{2,1,0:T(8,128)(2,1)} %param.3), channel_id=1, source_target_pairs={{0,4},{4,8},{8,12},{12,16},{16,20},{20,24},{24,28},{1,5},{5,9},{9,... | collective-permute-start | bytes 884744 | tf_op jit(solution)/shard_map/ppermute | solution.py:29
  12.6 16.2 %collective-permute-start.3 = (bf16[576,32]{1,0:T(8,128)(2,1)S(1)}, bf16[576,32]{1,0:T(8,128)(2,1)S(1)}, u32[]{:S(2)}, u32[]{:S(2)}) collective-permute-start(bf16[576,32]{1,0:T(8,128)(2,1)S(1)} %copy.14), channel_id=1, source_target_pairs={{0,3},{1,0},{2,1},{3,2},{4,7},{5,4},{6,5},{7,6},{8,11},{9,8},{10,9... | collective-permute-start | bytes 110600 | tf_op jit(solution)/shard_map/ppermute | solution.py:15
  16.6 23.1 %collective-permute-start.6 = (bf16[2,24,24,128]{3,2,1,0:T(8,128)(2,1)}, bf16[2,24,24,128]{3,2,1,0:T(8,128)(2,1)S(1)}, u32[]{:S(2)}, u32[]{:S(2)}) collective-permute-start(bf16[2,24,24,128]{3,2,1,0:T(8,128)(2,1)} %param.5), channel_id=1, source_target_pairs={{0,4},{4,8},{8,12},{12,16},{16,20},{20,24},{24,28},{1,5},{5,9},{9,... | collective-permute-start | bytes 884744 | tf_op jit(solution)/shard_map/ppermute | solution.py:29
  21.5 8.7 %copy-start.27 = (bf16[2,24,24,128]{3,2,1,0:T(8,128)(2,1)S(1)}, bf16[2,24,24,128]{3,2,1,0:T(8,128)(2,1)}, u32[]{:S(2)}) copy-start(bf16[2,24,24,128]{3,2,1,0:T(8,128)(2,1)} %param.5) | copy-start | bytes 884740
  22.9 39.3 %collective-permute-start.5 = (bf16[72,24,256]{2,1,0:T(8,128)(2,1)}, bf16[72,24,256]{2,1,0:T(8,128)(2,1)S(1)}, u32[]{:S(2)}, u32[]{:S(2)}) collective-permute-start(bf16[72,24,256]{2,1,0:T(8,128)(2,1)} %constant_dynamic-update-slice_fusion), channel_id=1, source_target_pairs={{1,0},{2,1},{3,2},{5,4},{6,5},{7,6},{9,8},{10,9},{11,10},{13,12},{... | collective-permute-start | bytes 2654216 | tf_op jit(solution)/shard_map/ppermute | solution.py:30
  24.2 38.0 %collective-permute-start.2 = (bf16[72,24,256]{2,1,0:T(8,128)(2,1)}, bf16[72,24,256]{2,1,0:T(8,128)(2,1)S(1)}, u32[]{:S(2)}, u32[]{:S(2)}) collective-permute-start(bf16[72,24,256]{2,1,0:T(8,128)(2,1)} %constant_dynamic-update-slice_fusion), channel_id=1, source_target_pairs={{0,1},{1,2},{2,3},{4,5},{5,6},{6,7},{8,9},{9,10},{10,11},{12,13},{... | collective-permute-start | bytes 2654216 | tf_op jit(solution)/shard_map/ppermute | solution.py:29
  29.6 6.3 %collective-permute-start.4 = (bf16[576,64]{1,0:T(8,128)(2,1)}, bf16[576,64]{1,0:T(8,128)(2,1)}, u32[]{:S(2)}, u32[]{:S(2)}) collective-permute-start(bf16[576,64]{1,0:T(8,128)(2,1)} %pad_maximum_fusion.17), channel_id=1, source_target_pairs={{0,2},{1,3},{2,0},{3,1},{4,6},{5,7},{6,4},{7,5},{8,10},{9,11},{10,... | collective-permute-start | bytes 221192 | tf_op jit(solution)/shard_map/ppermute | solution.py:15
  30.1 11.1 %collective-permute-start.7 = (bf16[2,24,24,128]{3,2,1,0:T(8,128)(2,1)S(1)}, bf16[2,24,24,128]{3,2,1,0:T(8,128)(2,1)S(1)}, u32[]{:S(2)}, u32[]{:S(2)}) collective-permute-start(bf16[2,24,24,128]{3,2,1,0:T(8,128)(2,1)S(1)} %copy-done.27), channel_id=1, source_target_pairs={{4,0},{8,4},{12,8},{16,12},{20,16},{24,20},{28,24},{5,1},{9,5},{13... | collective-permute-start | bytes 884744 | tf_op jit(solution)/shard_map/ppermute | solution.py:30
  39.6 87.5 %reduce-scatter.5.cloned.1.call-start = ((), (), s32[]{:S(2)}) async-start(), calls=%async_computation.3 | async-start | bytes 2654208 | tf_op jit(solution)/shard_map/reduce_scatter | solution.py:81
  42.0 40.3 %collective-permute-start.9 = (bf16[2,72,24,128]{3,2,1,0:T(8,128)(2,1)}, bf16[2,72,24,128]{3,2,1,0:T(8,128)(2,1)}, u32[]{:S(2)}, u32[]{:S(2)}) collective-permute-start(bf16[2,72,24,128]{3,2,1,0:T(8,128)(2,1)} %constant_dynamic-update-slice_fusion.3), channel_id=1, source_target_pairs={{0,1},{1,2},{2,3},{4,5},{5,6},{6,7},{8,9},{9,10},{10,11},{12,13},{... | collective-permute-start | bytes 2654216 | tf_op jit(solution)/shard_map/ppermute | solution.py:29
  60.1 44.3 %collective-permute-start.8 = (bf16[2,72,24,128]{3,2,1,0:T(8,128)(2,1)}, bf16[2,72,24,128]{3,2,1,0:T(8,128)(2,1)}, u32[]{:S(2)}, u32[]{:S(2)}) collective-permute-start(bf16[2,72,24,128]{3,2,1,0:T(8,128)(2,1)} %constant_dynamic-update-slice_fusion.3), channel_id=1, source_target_pairs={{1,0},{2,1},{3,2},{5,4},{6,5},{7,6},{9,8},{10,9},{11,10},{13,12},{... | collective-permute-start | bytes 2654216 | tf_op jit(solution)/shard_map/ppermute | solution.py:30
  62.2 3.7 %copy-start.25 = (bf16[24,24,256]{2,1,0:T(8,128)(2,1)S(1)}, bf16[24,24,256]{2,1,0:T(8,128)(2,1)}, u32[]{:S(2)}) copy-start(bf16[24,24,256]{2,1,0:T(8,128)(2,1)} %get-tuple-element.48) | copy-start | bytes 884740
  64.5 5.2 %copy-start.12 = (bf16[24,24,256]{2,1,0:T(8,128)(2,1)}, bf16[24,24,256]{2,1,0:T(8,128)(2,1)S(1)}, u32[]{:S(2)}) copy-start(bf16[24,24,256]{2,1,0:T(8,128)(2,1)S(1)} %get-tuple-element.34) | copy-start | bytes 884740
  64.5 5.2 %copy-start.18 = (bf16[24,24,256]{2,1,0:T(8,128)(2,1)}, bf16[24,24,256]{2,1,0:T(8,128)(2,1)S(1)}, u32[]{:S(2)}) copy-start(bf16[24,24,256]{2,1,0:T(8,128)(2,1)S(1)} %get-tuple-element.19) | copy-start | bytes 884740
  64.5 6.1 %copy-start.14 = (bf16[24,24,256]{2,1,0:T(8,128)(2,1)}, bf16[24,24,256]{2,1,0:T(8,128)(2,1)S(1)}, u32[]{:S(2)}) copy-start(bf16[24,24,256]{2,1,0:T(8,128)(2,1)S(1)} %get-tuple-element.33) | copy-start | bytes 884740
  64.5 8.0 %copy-start.16 = (bf16[24,24,256]{2,1,0:T(8,128)(2,1)}, bf16[24,24,256]{2,1,0:T(8,128)(2,1)S(1)}, u32[]{:S(2)}) copy-start(bf16[24,24,256]{2,1,0:T(8,128)(2,1)S(1)} %get-tuple-element.20) | copy-start | bytes 884740
  64.5 9.0 %copy-start.20 = (bf16[24,24,256]{2,1,0:T(8,128)(2,1)}, bf16[24,24,256]{2,1,0:T(8,128)(2,1)S(1)}, u32[]{:S(2)}) copy-start(bf16[24,24,256]{2,1,0:T(8,128)(2,1)S(1)} %get-tuple-element.38) | copy-start | bytes 884740
  64.6 10.9 %copy-start.2 = (bf16[24,24,256]{2,1,0:T(8,128)(2,1)}, bf16[24,24,256]{2,1,0:T(8,128)(2,1)S(1)}, u32[]{:S(2)}) copy-start(bf16[24,24,256]{2,1,0:T(8,128)(2,1)S(1)} %get-tuple-element.41) | copy-start | bytes 884740
  64.6 11.8 %copy-start.8 = (bf16[24,24,256]{2,1,0:T(8,128)(2,1)}, bf16[24,24,256]{2,1,0:T(8,128)(2,1)S(1)}, u32[]{:S(2)}) copy-start(bf16[24,24,256]{2,1,0:T(8,128)(2,1)S(1)} %get-tuple-element.37) | copy-start | bytes 884740
  64.6 13.7 %copy-start.4 = (bf16[24,24,256]{2,1,0:T(8,128)(2,1)}, bf16[24,24,256]{2,1,0:T(8,128)(2,1)S(1)}, u32[]{:S(2)}) copy-start(bf16[24,24,256]{2,1,0:T(8,128)(2,1)S(1)} %get-tuple-element.40) | copy-start | bytes 884740
  64.6 14.6 %copy-start.10 = (bf16[24,24,256]{2,1,0:T(8,128)(2,1)}, bf16[24,24,256]{2,1,0:T(8,128)(2,1)S(1)}, u32[]{:S(2)}) copy-start(bf16[24,24,256]{2,1,0:T(8,128)(2,1)S(1)} %get-tuple-element.36) | copy-start | bytes 884740
  64.6 16.5 %copy-start.6 = (bf16[24,24,256]{2,1,0:T(8,128)(2,1)}, bf16[24,24,256]{2,1,0:T(8,128)(2,1)S(1)}, u32[]{:S(2)}) copy-start(bf16[24,24,256]{2,1,0:T(8,128)(2,1)S(1)} %get-tuple-element.39) | copy-start | bytes 884740
  67.8 3.8 %copy-start.24 = (bf16[24,24,256]{2,1,0:T(8,128)(2,1)S(1)}, bf16[24,24,256]{2,1,0:T(8,128)(2,1)}, u32[]{:S(2)}) copy-start(bf16[24,24,256]{2,1,0:T(8,128)(2,1)} %get-tuple-element.50) | copy-start | bytes 884740
  70.7 3.8 %copy-start.23 = (bf16[24,24,256]{2,1,0:T(8,128)(2,1)S(1)}, bf16[24,24,256]{2,1,0:T(8,128)(2,1)}, u32[]{:S(2)}) copy-start(bf16[24,24,256]{2,1,0:T(8,128)(2,1)} %copy-done.22) | copy-start | bytes 884740
  82.1 69.8 %reduce-scatter.7.cloned.1.call-start = ((), (), s32[]{:S(2)}) async-start(), calls=%async_computation.4 | async-start | bytes 409600
  116.7 3.2 %copy-start.38 = (bf16[1,24,24,128]{3,2,1,0:T(8,128)(2,1)S(1)}, bf16[1,24,24,128]{3,2,1,0:T(8,128)(2,1)}, u32[]{:S(2)}) copy-start(bf16[1,24,24,128]{3,2,1,0:T(8,128)(2,1)} %get-tuple-element.26) | copy-start | bytes 442372
  117.8 3.2 %copy-start.37 = (bf16[1,24,24,128]{3,2,1,0:T(8,128)(2,1)S(1)}, bf16[1,24,24,128]{3,2,1,0:T(8,128)(2,1)}, u32[]{:S(2)}) copy-start(bf16[1,24,24,128]{3,2,1,0:T(8,128)(2,1)} %get-tuple-element.27) | copy-start | bytes 442372
  118.9 3.2 %copy-start.36 = (bf16[1,24,24,128]{3,2,1,0:T(8,128)(2,1)S(1)}, bf16[1,24,24,128]{3,2,1,0:T(8,128)(2,1)}, u32[]{:S(2)}) copy-start(bf16[1,24,24,128]{3,2,1,0:T(8,128)(2,1)} %get-tuple-element.28) | copy-start | bytes 442372
  127.1 3.0 %copy-start.43 = (bf16[1,24,24,128]{3,2,1,0:T(8,128)(2,1)S(1)}, bf16[1,24,24,128]{3,2,1,0:T(8,128)(2,1)}, u32[]{:S(2)}) copy-start(bf16[1,24,24,128]{3,2,1,0:T(8,128)(2,1)} %get-tuple-element.12) | copy-start | bytes 442372
  (25 other events, 39.3 us)
Sparse Core Ops, SparseCore 0:
  39.7 35.6 all-gather.1
  82.2 41.5 reduce-scatter.4
  129.2 22.6 reduce-scatter.6
